TPU v7x, 256 devices: a whole 4x4x8 slice. The times are simulated.
256 devices in a mesh: section: 16 (over y_hi, z), blk: 16 (over y_lo, x, core).
Axes of the slice: x: 4, y: 4 (y_hi: 2, y_lo: 2; y = y_hi * 2 + y_lo), z: 8, core: 2. Of those that a mesh axis runs over, the one named last changes fastest.
Arguments:
- waiting: bfloat16 [16, 512, 3072], P('section', 'blk'), may hold values from -12 to 12
- entering: bfloat16 [3, 512, 3072], P(None, 'blk'), may hold values from -12 to 12
- patch_order: int32 [12], replicated, may hold values from 0 to 11, each once
- step_index: int32 [1], replicated, may hold values from 0 to 27
- modulation: float32 [16, 28, 3, 3072], P('section'), may hold values from -4 to 4
- projection: bfloat16 [16, 3072, 3, 2048], P('section', None, None, 'blk'), may hold values from -0.109375 to 0.109375
- key_gain: float32 [16, 2048], P('section', 'blk'), may hold values from 2 to 3
- output_weight: bfloat16 [16, 2048, 3072], P('section', 'blk'), may hold values from -0.125 to 0.125
- stale_keys: bfloat16 [16, 12, 512, 2048], P('section', None, None, 'blk'), may hold values from -4 to 4
- stale_values: bfloat16 [16, 12, 512, 2048], P('section', None, None, 'blk'), may hold values from -4 to 4
Outputs:
- layer_out: bfloat16 [16, 4, 512, 3072], P('section', None, 'blk')
- fresh_kv: bfloat16 [16, 4, 512, 2, 2048], P('section', None, None, None, 'blk')
All inputs are finite; a program needn't handle non-finite values.
Results may differ from a plain program's by a relative error of at most 0.015.
Values may be sent and summed in bfloat16 or wider, within the bound.
No kernel may reach another device: no remote copies, remote signals or barrier semaphores. Data moves between devices by JAX's collectives and lax.ppermute only.
A program may use at most 128 MiB of HBM per device.

v0:
```python
import jax
import jax.numpy as jnp
from jax import lax
from jax.sharding import PartitionSpec as P

D = 3072
HD = 128
PATCHES = 12
TICKS = 4
STEPS = 28
epsilon = 1e-06


def passed_along(x, axis, by):
    size = lax.axis_size(axis)
    pairs = [(i, i + by) for i in range(size) if 0 <= i + by < size]
    return lax.ppermute(x, axis, pairs)


def root_norm(tensor):
    return tensor / jnp.sqrt(jnp.mean(tensor * tensor, axis=-1, keepdims=True) + epsilon)


def one_head(operands):
    head_q, head_k, head_v = operands
    logits = jnp.dot(head_q, head_k.T, preferred_element_type=jnp.float32) * HD ** (-0.5)
    exponent = jnp.exp(logits)
    weights = (exponent / jnp.sum(exponent, axis=-1, keepdims=True)).astype(jnp.bfloat16)
    return jnp.dot(weights, head_v, preferred_element_type=jnp.float32).astype(jnp.bfloat16)


def body(
    waiting,
    entering,
    patch_order,
    step_index,
    modulation,
    projection,
    key_gain,
    output_weight,
    stale_keys,
    stale_values,
):
    section_index = lax.axis_index("section")
    head_cols = projection.shape[3]
    heads_here = head_cols // HD
    selector = (jnp.arange(STEPS, dtype=jnp.int32) == step_index[0]).astype(jnp.float32)
    modulate = jnp.einsum("t,tcd->cd", selector, modulation[0], precision=lax.Precision.HIGHEST)
    flat_weight = projection[0].reshape(D, 3 * head_cols)
    key_scale = key_gain[0].reshape(heads_here, HD)
    out_matrix = output_weight[0]
    cache_k = stale_keys[0]
    cache_v = stale_values[0]
    produced_rows = []
    fresh_rows = []
    current = waiting[0]
    for tick_index in range(TICKS):
        if tick_index == 0:
            inflow = waiting[0]
        else:
            passed = passed_along(current, "section", 1)
            inflow = jnp.where(section_index == 0, entering[tick_index - 1], passed)
        inflow_wide = inflow.astype(jnp.float32)
        normed = (root_norm(inflow_wide) * (1.0 + modulate[1]) + modulate[0]).astype(jnp.bfloat16)
        projected = jnp.dot(
            lax.all_gather(normed, "blk", axis=0, tiled=True),
            flat_weight,
            preferred_element_type=jnp.float32,
        )
        tokens = projected.shape[0]
        projected = projected.reshape(tokens, 3, heads_here, HD)
        queries = root_norm(projected[:, 0]).astype(jnp.bfloat16)
        keys_new = (root_norm(projected[:, 1]) * key_scale).astype(jnp.bfloat16)
        values_new = projected[:, 2].astype(jnp.bfloat16)
        position = jnp.mod(tick_index - section_index, PATCHES)
        patch_slot = lax.dynamic_index_in_dim(patch_order, position, 0, keepdims=False)
        anchor = jnp.zeros((), jnp.int32)
        corner = (patch_slot, anchor, anchor)
        keys_flat = keys_new.reshape(tokens, head_cols)
        values_flat = values_new.reshape(tokens, head_cols)
        cache_k = lax.dynamic_update_slice(cache_k, keys_flat.reshape(1, tokens, head_cols), corner)
        cache_v = lax.dynamic_update_slice(
            cache_v, values_flat.reshape(1, tokens, head_cols), corner
        )
        keys_heads = cache_k.reshape(PATCHES * tokens, heads_here, HD).transpose(1, 0, 2)
        values_heads = cache_v.reshape(PATCHES * tokens, heads_here, HD).transpose(1, 0, 2)
        attended = lax.map(one_head, (queries.transpose(1, 0, 2), keys_heads, values_heads))
        attended = attended.transpose(1, 0, 2).reshape(tokens, head_cols)
        attention = lax.psum_scatter(
            jnp.dot(attended, out_matrix, preferred_element_type=jnp.float32).astype(jnp.bfloat16),
            "blk",
            scatter_dimension=0,
            tiled=True,
        ).astype(jnp.float32)
        current = (inflow_wide + modulate[2] * attention).astype(jnp.bfloat16)
        produced_rows.append(current)
        fresh_rows.append(jnp.stack([keys_flat, values_flat], axis=1))
    layer_out = jnp.stack(produced_rows)[None]
    fresh_kv = jnp.stack(fresh_rows)[None]
    return (layer_out, fresh_kv)


def solution(mesh):
    placed = (
        P("section", "blk", None),
        P(None, "blk", None),
        P(),
        P(),
        P("section", None, None, None),
        P("section", None, None, "blk"),
        P("section", "blk"),
        P("section", "blk", None),
        P("section", None, None, "blk"),
        P("section", None, None, "blk"),
    )
    return jax.shard_map(
        body,
        mesh=mesh,
        in_specs=placed,
        out_specs=(P("section", None, "blk", None), P("section", None, None, None, "blk")),
        check_vma=False,
    )
```

profile of v0, /device:TPU:32, one launch (start us, length us, event | category | flops | bytes accessed | tf_op | source)
XLA Modules:
  0.0 570.3 jit_solution(17247065414648931700)
XLA Ops:
  8.1 0.5 copy-done.17
  8.6 0.6 fusion.35
  9.2 0.6 fusion.115
  10.0 0.8 fusion.64
  11.0 0.7 fusion.116
  12.9 2.5 copy.15
  16.1 35.7 %all-gather.5.cloned.1.call-done = bf16[512,3072]{1,0:T(8,128)(2,1)} async-done(((bf16[32,3072]{1,0:T(8,128)(2,1)}), bf16[512,3072]{1,0:T(8,128)(2,1)}) %all-gather.5.cloned.1.call-update) | async-done | bytes 3145744 | tf_op jit(solution)/shard_map/all_gather | solution.py:66
  51.8 4.5 fusion.14
  56.9 5.7 %fusion = (f32[512]{0:T(512)S(1)}, f32[512,6144]{1,0:T(8,128)}) fusion(bf16[6144,128]{1,0:T(8,128)(2,1)S(1)} %bitcast.227, f32[512]{0:T(512)S(1)} %add_sqrt_fusion.7, f32[512,3,1,128]{3,0,1,2:T(8,128)S(1)} %bitcast.236), kind=kOutput, calls=%fused_computation.8 | convolution fusion | flops 811728384 | bytes 14422016 | tf_op jit(solution)/shard_map/while/body/eval_jaxpr/dot_general | solution.py:26
  62.6 11.0 %convolution_convert_fusion.3 = bf16[512,3072]{1,0:T(8,128)(2,1)} fusion(bf16[6144,128]{1,0:T(8,128)(2,1)} %bitcast.239, f32[512,6144]{1,0:T(8,128)} %get-tuple-element.90, f32[512]{0:T(512)S(1)} %get-tuple-element.89, bf16[1,128,3072]{2,1,0:T(8,128)(2,1)S(1)} %copy-done), kind=kOutput, calls=%fused_computation.19 | convolution fusion | flops 1219035136 | bytes 18089984 | tf_op jit(solution)/shard_map/dot_general | solution.py:90
  73.7 67.9 %reduce-scatter.5.cloned.1.call-done = bf16[32,3072]{1,0:T(8,128)(2,1)} async-done(((bf16[512,3072]{1,0:T(8,128)(2,1)}), bf16[32,3072]{1,0:T(8,128)(2,1)}) %reduce-scatter.5.cloned.1.call-update) | async-done | bytes 196624 | tf_op jit(solution)/shard_map/reduce_scatter | solution.py:89
  141.6 1.0 fusion.65
  142.6 3.5 collective-permute-start
  146.1 4.2 collective-permute-done
  150.3 1.2 fusion.46
  151.5 1.5 fusion.49
  155.2 36.0 %all-gather.7.cloned.1.call-done = bf16[512,3072]{1,0:T(8,128)(2,1)} async-done(((bf16[32,3072]{1,0:T(8,128)(2,1)}), bf16[512,3072]{1,0:T(8,128)(2,1)}) %all-gather.7.cloned.1.call-update) | async-done | bytes 3145744 | tf_op jit(solution)/shard_map/all_gather | solution.py:66
  191.3 4.5 fusion.20
  196.4 0.4 copy-done.24
  196.7 6.3 %fusion.1 = (f32[512]{0:T(512)}, f32[512,6144]{1,0:T(8,128)}) fusion(bf16[6144,128]{1,0:T(8,128)(2,1)S(1)} %bitcast.228, f32[512]{0:T(512)S(1)} %add_sqrt_fusion.5, f32[512,3,1,128]{3,0,2,1:T(8,128)S(1)} %fusion.20), kind=kOutput, calls=%fused_computation.9 | convolution fusion | flops 811728384 | bytes 14422016 | tf_op jit(solution)/shard_map/while/body/eval_jaxpr/dot_general | solution.py:26
  203.0 11.0 %convolution_convert_fusion.2 = bf16[512,3072]{1,0:T(8,128)(2,1)} fusion(bf16[6144,128]{1,0:T(8,128)(2,1)} %bitcast.240, f32[512,6144]{1,0:T(8,128)} %get-tuple-element.92, f32[512]{0:T(512)} %get-tuple-element.91, bf16[1,128,3072]{2,1,0:T(8,128)(2,1)S(1)} %copy-done), kind=kOutput, calls=%fused_computation.18 | convolution fusion | flops 1219035136 | bytes 18089984 | tf_op jit(solution)/shard_map/dot_general | solution.py:90
  214.1 67.9 %reduce-scatter.7.cloned.1.call-done = bf16[32,3072]{1,0:T(8,128)(2,1)} async-done(((bf16[512,3072]{1,0:T(8,128)(2,1)}), bf16[32,3072]{1,0:T(8,128)(2,1)}) %reduce-scatter.7.cloned.1.call-update) | async-done | bytes 196624 | tf_op jit(solution)/shard_map/reduce_scatter | solution.py:89
  282.0 1.0 fusion.50
  283.0 3.5 collective-permute-start.1
  286.5 4.1 collective-permute-done.1
  290.6 1.1 fusion.51
  291.7 1.5 fusion.54
  295.6 35.9 %all-gather.9.cloned.1.call-done = bf16[512,3072]{1,0:T(8,128)(2,1)} async-done(((bf16[32,3072]{1,0:T(8,128)(2,1)}), bf16[512,3072]{1,0:T(8,128)(2,1)}) %all-gather.9.cloned.1.call-update) | async-done | bytes 3145744 | tf_op jit(solution)/shard_map/all_gather | solution.py:66
  331.5 4.5 fusion.25
  336.9 6.3 %fusion.2 = (f32[512]{0:T(512)}, f32[512,6144]{1,0:T(8,128)}) fusion(bf16[6144,128]{1,0:T(8,128)(2,1)S(1)} %bitcast.229, f32[512]{0:T(512)S(1)} %add_sqrt_fusion.3, f32[512,3,1,128]{3,0,2,1:T(8,128)S(1)} %fusion.25), kind=kOutput, calls=%fused_computation.10 | convolution fusion | flops 811728384 | bytes 14422016 | tf_op jit(solution)/shard_map/while/body/eval_jaxpr/dot_general | solution.py:26
  343.2 11.0 %convolution_convert_fusion.1 = bf16[512,3072]{1,0:T(8,128)(2,1)} fusion(bf16[6144,128]{1,0:T(8,128)(2,1)} %bitcast.241, f32[512,6144]{1,0:T(8,128)} %get-tuple-element.94, f32[512]{0:T(512)} %get-tuple-element.93, bf16[1,128,3072]{2,1,0:T(8,128)(2,1)S(1)} %copy-done), kind=kOutput, calls=%fused_computation.17 | convolution fusion | flops 1219035136 | bytes 18089984 | tf_op jit(solution)/shard_map/dot_general | solution.py:90
  354.3 67.9 %reduce-scatter.9.cloned.1.call-done = bf16[32,3072]{1,0:T(8,128)(2,1)} async-done(((bf16[512,3072]{1,0:T(8,128)(2,1)}), bf16[32,3072]{1,0:T(8,128)(2,1)}) %reduce-scatter.9.cloned.1.call-update) | async-done | bytes 196624 | tf_op jit(solution)/shard_map/reduce_scatter | solution.py:89
  422.2 1.0 fusion.55
  423.2 3.5 collective-permute-start.2
  426.7 4.1 collective-permute-done.2
  430.8 1.1 fusion.56
  431.9 1.5 fusion.59
  435.5 36.1 %all-gather.11.cloned.1.call-done = bf16[512,3072]{1,0:T(8,128)(2,1)} async-done(((bf16[32,3072]{1,0:T(8,128)(2,1)}), bf16[512,3072]{1,0:T(8,128)(2,1)}) %all-gather.11.cloned.1.call-update) | async-done | bytes 3145744 | tf_op jit(solution)/shard_map/all_gather | solution.py:66
  471.7 4.5 fusion.30
  476.7 5.7 %fusion.3 = (f32[512]{0:T(512)S(1)}, f32[512,6144]{1,0:T(8,128)}) fusion(bf16[6144,128]{1,0:T(8,128)(2,1)S(1)} %bitcast.230, f32[512]{0:T(512)S(1)} %add_sqrt_fusion.1, f32[512,3,1,128]{3,0,2,1:T(8,128)S(1)} %fusion.30), kind=kOutput, calls=%fused_computation.11 | convolution fusion | flops 811728384 | bytes 14422016 | tf_op jit(solution)/shard_map/while/body/eval_jaxpr/dot_general | solution.py:26
  482.5 11.0 %convolution_convert_fusion = bf16[512,3072]{1,0:T(8,128)(2,1)} fusion(bf16[6144,128]{1,0:T(8,128)(2,1)} %bitcast.242, f32[512,6144]{1,0:T(8,128)} %get-tuple-element.96, f32[512]{0:T(512)S(1)} %get-tuple-element.95, bf16[1,128,3072]{2,1,0:T(8,128)(2,1)S(1)} %copy-done), kind=kOutput, calls=%fused_computation.16 | convolution fusion | flops 1219035136 | bytes 18089984 | tf_op jit(solution)/shard_map/dot_general | solution.py:90
  493.5 1.1 copy-done.3
  494.8 1.0 fusion.102
  495.8 1.3 fusion.83
  497.5 2.0 copy.17
  499.5 62.0 %reduce-scatter.11.cloned.1.call-done = bf16[32,3072]{1,0:T(8,128)(2,1)} async-done(((bf16[512,3072]{1,0:T(8,128)(2,1)}), bf16[32,3072]{1,0:T(8,128)(2,1)}) %reduce-scatter.11.cloned.1.call-update) | async-done | bytes 196624 | tf_op jit(solution)/shard_map/reduce_scatter | solution.py:89
  561.5 1.0 fusion.86
  562.5 1.0 maximum_bitcast_fusion.1
  (113 shorter events, 4.3 us)
Async XLA Ops:
  7.2 55.5 %copy-start = (bf16[1,128,3072]{2,1,0:T(8,128)(2,1)S(1)}, bf16[1,128,3072]{2,1,0:T(8,128)(2,1)}, u32[]{:S(2)}) copy-start(bf16[1,128,3072]{2,1,0:T(8,128)(2,1)} %param.17) | copy-start | bytes 2359300
  7.2 2.6 copy-start.8
  7.2 44.6 %all-gather.5.cloned.1.call-start = ((), (), s32[]{:S(2)}) async-start(), calls=%async_computation.4 | async-start | bytes 3342336 | tf_op jit(solution)/shard_map/all_gather | solution.py:66
  7.2 1.3 copy-start.17
  7.2 3.7 copy-start.32
  7.3 5.6 copy-start.7
  9.8 46.6 %copy-start.22 = (f32[1,3072]{1,0:T(1,128)}, f32[1,3072]{1,0:T(1,128)S(1)}, u32[]{:S(2)}) copy-start(f32[1,3072]{1,0:T(1,128)S(1)} %get-tuple-element.80) | copy-start | bytes 36868
  10.8 130.8 %reduce-scatter.5.cloned.1.call-start = ((), (), s32[]{:S(2)}) async-start(), calls=%async_computation.5 | async-start | bytes 3342336 | tf_op jit(solution)/shard_map/reduce_scatter | solution.py:89
  16.0 40.7 %copy-start.1 = (bf16[1,12,512,128]{3,2,1,0:T(8,128)(2,1)S(1)}, bf16[1,12,512,128]{3,2,1,0:T(8,128)(2,1)}, u32[]{:S(2)}) copy-start(bf16[1,12,512,128]{3,2,1,0:T(8,128)(2,1)} %param.18) | copy-start | bytes 4718596
  16.0 40.7 %copy-start.28 = (f32[1,128]{1,0:T(1,128)S(1)}, f32[1,128]{1,0:T(1,128)}, u32[]{:S(2)}) copy-start(f32[1,128]{1,0:T(1,128)} %param.16) | copy-start | bytes 1540
  51.8 4.9 copy-start.16
  56.9 5.7 %copy-start.9 = (bf16[12,512,128]{2,1,0:T(8,128)(2,1)}, bf16[12,512,128]{2,1,0:T(8,128)(2,1)S(1)}, u32[]{:S(2)}) copy-start(bf16[12,512,128]{2,1,0:T(8,128)(2,1)S(1)} %get-tuple-element.98) | copy-start | bytes 4718596
  73.6 117.6 %all-gather.7.cloned.1.call-start = ((), (), s32[]{:S(2)}) async-start(), calls=%async_computation.6 | async-start | bytes 3342336 | tf_op jit(solution)/shard_map/all_gather | solution.py:66
  142.6 7.7 %collective-permute-start = (bf16[32,3072]{1,0:T(8,128)(2,1)S(1)}, bf16[32,3072]{1,0:T(8,128)(2,1)}, u32[]{:S(2)}, u32[]{:S(2)}) collective-permute-start(bf16[32,3072]{1,0:T(8,128)(2,1)S(1)} %fusion.65), channel_id=1, source_target_pairs={{0,16},{16,32},{32,48},{48,64},{64,80},{80,96},{96,112},{112,128},... | collective-permute-start | bytes 589832 | tf_op jit(solution)/shard_map/ppermute | solution.py:17
  153.1 129.0 %reduce-scatter.7.cloned.1.call-start = ((), (), s32[]{:S(2)}) async-start(), calls=%async_computation.7 | async-start | bytes 3342336 | tf_op jit(solution)/shard_map/reduce_scatter | solution.py:89
  191.3 4.9 copy-start.10
  191.3 4.9 copy-start.29
  195.8 7.2 %copy-start.2 = (f32[512,3,1,128]{3,0,2,1:T(8,128)}, f32[512,3,1,128]{3,0,2,1:T(8,128)S(1)}, u32[]{:S(2)}) copy-start(f32[512,3,1,128]{3,0,2,1:T(8,128)S(1)} %fusion.20) | copy-start | bytes 2359300
  196.1 0.6 copy-start.24
  196.7 6.3 %copy-start.11 = (bf16[12,512,128]{2,1,0:T(8,128)(2,1)}, bf16[12,512,128]{2,1,0:T(8,128)(2,1)S(1)}, u32[]{:S(2)}) copy-start(bf16[12,512,128]{2,1,0:T(8,128)(2,1)S(1)} %get-tuple-element.72) | copy-start | bytes 4718596
  214.0 117.4 %all-gather.9.cloned.1.call-start = ((), (), s32[]{:S(2)}) async-start(), calls=%async_computation.8 | async-start | bytes 3342336 | tf_op jit(solution)/shard_map/all_gather | solution.py:66
  283.0 3.5 copy-start.18
  283.0 7.6 %collective-permute-start.1 = (bf16[32,3072]{1,0:T(8,128)(2,1)S(1)}, bf16[32,3072]{1,0:T(8,128)(2,1)S(1)}, u32[]{:S(2)}, u32[]{:S(2)}) collective-permute-start(bf16[32,3072]{1,0:T(8,128)(2,1)S(1)} %fusion.50), channel_id=1, source_target_pairs={{0,16},{16,32},{32,48},{48,64},{64,80},{80,96},{96,112},{112,128},... | collective-permute-start | bytes 589832 | tf_op jit(solution)/shard_map/ppermute | solution.py:17
  293.3 129.0 %reduce-scatter.9.cloned.1.call-start = ((), (), s32[]{:S(2)}) async-start(), calls=%async_computation.9 | async-start | bytes 3342336 | tf_op jit(solution)/shard_map/reduce_scatter | solution.py:89
  331.5 4.9 copy-start.12
  331.5 4.9 copy-start.30
  336.0 7.2 %copy-start.4 = (f32[512,3,1,128]{3,0,2,1:T(8,128)}, f32[512,3,1,128]{3,0,2,1:T(8,128)S(1)}, u32[]{:S(2)}) copy-start(f32[512,3,1,128]{3,0,2,1:T(8,128)S(1)} %fusion.25) | copy-start | bytes 2359300
  336.3 0.6 copy-start.26
  336.9 6.3 %copy-start.13 = (bf16[12,512,128]{2,1,0:T(8,128)(2,1)}, bf16[12,512,128]{2,1,0:T(8,128)(2,1)S(1)}, u32[]{:S(2)}) copy-start(bf16[12,512,128]{2,1,0:T(8,128)(2,1)S(1)} %get-tuple-element.70) | copy-start | bytes 4718596
  354.2 117.4 %all-gather.11.cloned.1.call-start = ((), (), s32[]{:S(2)}) async-start(), calls=%async_computation.10 | async-start | bytes 3342336 | tf_op jit(solution)/shard_map/all_gather | solution.py:66
  423.2 3.5 copy-start.20
  423.2 7.6 %collective-permute-start.2 = (bf16[32,3072]{1,0:T(8,128)(2,1)S(1)}, bf16[32,3072]{1,0:T(8,128)(2,1)S(1)}, u32[]{:S(2)}, u32[]{:S(2)}) collective-permute-start(bf16[32,3072]{1,0:T(8,128)(2,1)S(1)} %fusion.55), channel_id=1, source_target_pairs={{0,16},{16,32},{32,48},{48,64},{64,80},{80,96},{96,112},{112,128},... | collective-permute-start | bytes 589832 | tf_op jit(solution)/shard_map/ppermute | solution.py:17
  433.5 128.0 %reduce-scatter.11.cloned.1.call-start = ((), (), s32[]{:S(2)}) async-start(), calls=%async_computation.11 | async-start | bytes 3342336 | tf_op jit(solution)/shard_map/reduce_scatter | solution.py:89
  435.5 41.0 %copy-start.31 = (f32[1,128]{1,0:T(1,128)S(1)}, f32[1,128]{1,0:T(1,128)}, u32[]{:S(2)}) copy-start(f32[1,128]{1,0:T(1,128)} %param.16) | copy-start | bytes 1540
  471.6 4.9 copy-start.14
  476.2 6.3 %copy-start.6 = (f32[512,3,1,128]{3,0,2,1:T(8,128)}, f32[512,3,1,128]{3,0,2,1:T(8,128)S(1)}, u32[]{:S(2)}) copy-start(f32[512,3,1,128]{3,0,2,1:T(8,128)S(1)} %fusion.30) | copy-start | bytes 2359300
  476.7 5.7 %copy-start.15 = (bf16[12,512,128]{2,1,0:T(8,128)(2,1)}, bf16[12,512,128]{2,1,0:T(8,128)(2,1)S(1)}, u32[]{:S(2)}) copy-start(bf16[12,512,128]{2,1,0:T(8,128)(2,1)S(1)} %get-tuple-element.63) | copy-start | bytes 4718596
  493.4 1.1 copy-start.3
  493.4 1.4 copy-start.5
  493.4 2.4 copy-start.25
  493.4 2.4 copy-start.27
  497.1 64.3 %copy-start.23 = (f32[1,3072]{1,0:T(1,128)S(1)}, f32[1,3072]{1,0:T(1,128)}, u32[]{:S(2)}) copy-start(f32[1,3072]{1,0:T(1,128)} %get-tuple-element.73) | copy-start | bytes 36868
  497.2 65.3 %copy-start.19 = (bf16[32,3072]{1,0:T(8,128)(2,1)S(1)}, bf16[32,3072]{1,0:T(8,128)(2,1)}, u32[]{:S(2)}) copy-start(bf16[32,3072]{1,0:T(8,128)(2,1)} %copy-done.18) | copy-start | bytes 589828
  497.2 65.3 %copy-start.21 = (bf16[32,3072]{1,0:T(8,128)(2,1)S(1)}, bf16[32,3072]{1,0:T(8,128)(2,1)}, u32[]{:S(2)}) copy-start(bf16[32,3072]{1,0:T(8,128)(2,1)} %copy-done.20) | copy-start | bytes 589828
Sparse Core Ops, SparseCore 0:
  10.9 40.8 all-gather.4
  73.8 67.8 reduce-scatter.4
  153.2 38.0 all-gather.6
  214.2 67.8 reduce-scatter.6
  293.4 38.0 all-gather.8
  354.4 67.8 reduce-scatter.8
  433.6 38.0 all-gather.10
  493.6 67.8 reduce-scatter.10
where the time goes:
time: 571 us; the launch traced here: 570 us
  waiting for transfers between devices  422 us (74%)
  matrix products  86.7 us (15%)
  between operations  23.2 us (4%)
  other arithmetic  18.1 us (3%)
  starting transfers between devices  11.4 us (2%)
  local copies, waits for them, and re-layouts  8.91 us (2%)
    reduce_scatter x4, waiting for transfers between devices, body(): lax.psum_scatter(jnp.dot(attended, out_matrix, preferred_element_type=jnp...  266 us
    all_gather x4, waiting for transfers between devices, body(): lax.all_gather(normed, 'blk', axis=0, tiled=True)  144 us
    dot_general x4, matrix products, body(): jnp.dot(attended, out_matrix, preferred_element_type=jnp.float32)  43.9 us
    dot_general x4, matrix products, one_head(): jnp.dot(head_q, head_k.T, preferred_element_type=jnp.float32) * HD ** (-0.5)  24 us
    dot_general x4, matrix products, body(): jnp.dot(lax.all_gather(normed, 'blk', axis=0, tiled=True), flat_weight, p...  18.1 us
    ppermute x3, waiting for transfers between devices, passed_along(): return lax.ppermute(x, axis, pairs)  12.4 us
  transfers between devices with their start and end apart: 11, of which 11 were waited for; matrix products, arithmetic and copies ran while one was open for 1% of the time, Pallas kernels for 0%

commit v1 on v0

--- a/solution.py
+++ b/solution.py
@@ -9,6 +9,13 @@
 TICKS = 4
 STEPS = 28
 epsilon = 1e-06
+
+
+def all_by_exchange(value, name, d):
+    devices = lax.axis_size(name)
+    shards = jnp.stack([value for _ in range(devices)])
+    shards = lax.all_to_all(shards, name, split_axis=0, concat_axis=0)
+    return jnp.concatenate(shards, axis=d)
 
 
 def passed_along(x, axis, by):
@@ -63,9 +70,7 @@
         inflow_wide = inflow.astype(jnp.float32)
         normed = (root_norm(inflow_wide) * (1.0 + modulate[1]) + modulate[0]).astype(jnp.bfloat16)
         projected = jnp.dot(
-            lax.all_gather(normed, "blk", axis=0, tiled=True),
-            flat_weight,
-            preferred_element_type=jnp.float32,
+            all_by_exchange(normed, "blk", 0), flat_weight, preferred_element_type=jnp.float32
         )
         tokens = projected.shape[0]
         projected = projected.reshape(tokens, 3, heads_here, HD)

time: 571 us -> 615 us (1.077)
  waiting for transfers between devices: 422 us -> 441 us
  starting transfers between devices: 11.4 us -> 30.3 us
  local copies, waits for them, and re-layouts: 8.91 us -> 17.2 us
    all_to_all x0 -> x4, waiting for transfers between devices: none -> 157 us  [all_by_exchange(): shards = lax.all_to_all(shards, name, split_axis=0, concat_axis=0)]
    all_gather x4 -> x0, waiting for transfers between devices: 144 us -> none  [body(): lax.all_gather(normed, 'blk', axis=0, tiled=True)]
    all_to_all x0 -> x4, starting transfers between devices: none -> 19 us  [all_by_exchange(): shards = lax.all_to_all(shards, name, split_axis=0, concat_axis=0)]
    another operation x0 -> x4, local copies, waits for them, and re-layouts: none -> 8.26 us  [all_by_exchange(): shards = jnp.stack([value for _ in range(devices)])]
where the time goes in v1:
time: 615 us; the launch traced here: 614 us
  waiting for transfers between devices  441 us (72%)
  matrix products  86.6 us (14%)
  starting transfers between devices  30.3 us (5%)
  between operations  22.8 us (4%)
  local copies, waits for them, and re-layouts  17.2 us (3%)
  other arithmetic  15.4 us (3%)
    reduce_scatter x4, waiting for transfers between devices, body(): lax.psum_scatter(jnp.dot(attended, out_matrix, preferred_element_type=jnp...  272 us
    all_to_all x4, waiting for transfers between devices, all_by_exchange(): shards = lax.all_to_all(shards, name, split_axis=0, concat_axis=0)  157 us
    dot_general x4, matrix products, body(): jnp.dot(attended, out_matrix, preferred_element_type=jnp.float32)  43.9 us
    dot_general x4, matrix products, one_head(): jnp.dot(head_q, head_k.T, preferred_element_type=jnp.float32) * HD ** (-0.5)  24 us
    all_to_all x4, starting transfers between devices, all_by_exchange(): shards = lax.all_to_all(shards, name, split_axis=0, concat_axis=0)  19 us
    dot_general x4, matrix products, body(): jnp.dot(all_by_exchange(normed, 'blk', 0), flat_weight, preferred_element...  18.2 us
    ppermute x3, waiting for transfers between devices, passed_along(): return lax.ppermute(x, axis, pairs)  12.4 us
  transfers between devices with their start and end apart: 11, of which 11 were waited for; matrix products, arithmetic and copies ran while one was open for 1% of the time, Pallas kernels for 0%

profile of v1, /device:TPU:32, one launch (start us, length us, event | category | flops | bytes accessed | tf_op | source)
XLA Modules:
  0.0 613.7 jit_solution(9949643212134116306)
XLA Ops:
  10.1 2.1 stack.39
  12.1 5.6 all-to-all-start
  19.9 2.5 copy.15
  23.1 37.0 %all-to-all-done = bf16[16,32,3072]{2,1,0:T(8,128)(2,1)} async-done(((bf16[16,32,3072]{2,1,0:T(8,128)(2,1)}), bf16[16,32,3072]{2,1,0:T(8,128)(2,1)}, u32[]{:S(2)}, u32[]{:S(2)}) %all-to-all-start) | async-done | bytes 3145760 | tf_op jit(solution)/shard_map/all_to_all | solution.py:17
  60.2 4.6 fusion.14
  65.3 5.7 fusion
  71.0 11.0 %convolution_convert_fusion.3 = bf16[512,3072]{1,0:T(8,128)(2,1)} fusion(bf16[6144,128]{1,0:T(8,128)(2,1)} %bitcast.244, f32[512,6144]{1,0:T(8,128)} %get-tuple-element.90, f32[512]{0:T(512)S(1)} %get-tuple-element.89, bf16[1,128,3072]{2,1,0:T(8,128)(2,1)S(1)} %copy-done), kind=kOutput, calls=%fused_computation.19 | convolution fusion | flops 1219035136 | bytes 18089984 | tf_op jit(solution)/shard_map/dot_general | solution.py:95
  82.0 69.5 %reduce-scatter.5.cloned.1.call-done = bf16[32,3072]{1,0:T(8,128)(2,1)} async-done(((bf16[512,3072]{1,0:T(8,128)(2,1)}), bf16[32,3072]{1,0:T(8,128)(2,1)}) %reduce-scatter.5.cloned.1.call-update) | async-done | bytes 196624 | tf_op jit(solution)/shard_map/reduce_scatter | solution.py:94
  151.5 1.0 fusion.39
  152.5 3.5 collective-permute-start
  156.0 4.2 collective-permute-done
  160.2 1.2 fusion.43
  161.4 0.8 fusion.46
  162.3 2.1 stack.41
  164.3 4.5 all-to-all-start.1
  171.0 40.0 %all-to-all-done.1 = bf16[16,32,3072]{2,1,0:T(8,128)(2,1)} async-done(((bf16[16,32,3072]{2,1,0:T(8,128)(2,1)}), bf16[16,32,3072]{2,1,0:T(8,128)(2,1)}, u32[]{:S(2)}, u32[]{:S(2)}) %all-to-all-start.1) | async-done | bytes 3145760 | tf_op jit(solution)/shard_map/all_to_all | solution.py:17
  211.0 4.5 fusion.16
  216.5 6.3 %fusion.1 = (f32[512]{0:T(512)}, f32[512,6144]{1,0:T(8,128)}) fusion(bf16[6144,128]{1,0:T(8,128)(2,1)S(1)} %bitcast.233, f32[512]{0:T(512)S(1)} %add_sqrt_fusion.5, f32[512,3,1,128]{3,0,2,1:T(8,128)S(1)} %fusion.16), kind=kOutput, calls=%fused_computation.9 | convolution fusion | flops 811728384 | bytes 14422016 | tf_op jit(solution)/shard_map/while/body/eval_jaxpr/dot_general | solution.py:33
  222.8 11.0 %convolution_convert_fusion.2 = bf16[512,3072]{1,0:T(8,128)(2,1)} fusion(bf16[6144,128]{1,0:T(8,128)(2,1)} %bitcast.245, f32[512,6144]{1,0:T(8,128)} %get-tuple-element.92, f32[512]{0:T(512)} %get-tuple-element.91, bf16[1,128,3072]{2,1,0:T(8,128)(2,1)S(1)} %copy-done), kind=kOutput, calls=%fused_computation.18 | convolution fusion | flops 1219035136 | bytes 18089984 | tf_op jit(solution)/shard_map/dot_general | solution.py:95
  233.8 69.4 %reduce-scatter.7.cloned.1.call-done = bf16[32,3072]{1,0:T(8,128)(2,1)} async-done(((bf16[512,3072]{1,0:T(8,128)(2,1)}), bf16[32,3072]{1,0:T(8,128)(2,1)}) %reduce-scatter.7.cloned.1.call-update) | async-done | bytes 196624 | tf_op jit(solution)/shard_map/reduce_scatter | solution.py:94
  303.2 1.0 fusion.47
  304.2 3.4 collective-permute-start.1
  307.7 4.1 collective-permute-done.1
  311.8 1.1 fusion.48
  313.7 2.1 stack.43
  315.8 4.5 all-to-all-start.2
  322.3 40.2 %all-to-all-done.2 = bf16[16,32,3072]{2,1,0:T(8,128)(2,1)} async-done(((bf16[16,32,3072]{2,1,0:T(8,128)(2,1)}), bf16[16,32,3072]{2,1,0:T(8,128)(2,1)}, u32[]{:S(2)}, u32[]{:S(2)}) %all-to-all-start.2) | async-done | bytes 3145760 | tf_op jit(solution)/shard_map/all_to_all | solution.py:17
  362.5 4.5 fusion.19
  368.0 6.3 %fusion.2 = (f32[512]{0:T(512)}, f32[512,6144]{1,0:T(8,128)}) fusion(bf16[6144,128]{1,0:T(8,128)(2,1)S(1)} %bitcast.234, f32[512]{0:T(512)S(1)} %add_sqrt_fusion.3, f32[512,3,1,128]{3,0,2,1:T(8,128)S(1)} %fusion.19), kind=kOutput, calls=%fused_computation.10 | convolution fusion | flops 811728384 | bytes 14422016 | tf_op jit(solution)/shard_map/while/body/eval_jaxpr/dot_general | solution.py:33
  374.3 11.0 %convolution_convert_fusion.1 = bf16[512,3072]{1,0:T(8,128)(2,1)} fusion(bf16[6144,128]{1,0:T(8,128)(2,1)} %bitcast.246, f32[512,6144]{1,0:T(8,128)} %get-tuple-element.94, f32[512]{0:T(512)} %get-tuple-element.93, bf16[1,128,3072]{2,1,0:T(8,128)(2,1)S(1)} %copy-done), kind=kOutput, calls=%fused_computation.17 | convolution fusion | flops 1219035136 | bytes 18089984 | tf_op jit(solution)/shard_map/dot_general | solution.py:95
  385.3 69.4 %reduce-scatter.9.cloned.1.call-done = bf16[32,3072]{1,0:T(8,128)(2,1)} async-done(((bf16[512,3072]{1,0:T(8,128)(2,1)}), bf16[32,3072]{1,0:T(8,128)(2,1)}) %reduce-scatter.9.cloned.1.call-update) | async-done | bytes 196624 | tf_op jit(solution)/shard_map/reduce_scatter | solution.py:94
  454.7 1.0 fusion.52
  455.7 3.5 collective-permute-start.2
  459.2 4.1 collective-permute-done.2
  463.2 1.1 fusion.53
  465.2 2.1 stack.45
  467.3 4.5 all-to-all-start.3
  473.9 40.0 %all-to-all-done.3 = bf16[16,32,3072]{2,1,0:T(8,128)(2,1)} async-done(((bf16[16,32,3072]{2,1,0:T(8,128)(2,1)}), bf16[16,32,3072]{2,1,0:T(8,128)(2,1)}, u32[]{:S(2)}, u32[]{:S(2)}) %all-to-all-start.3) | async-done | bytes 3145760 | tf_op jit(solution)/shard_map/all_to_all | solution.py:17
  514.0 4.5 fusion.22
  519.1 5.7 fusion.3
  524.8 11.0 %convolution_convert_fusion = bf16[512,3072]{1,0:T(8,128)(2,1)} fusion(bf16[6144,128]{1,0:T(8,128)(2,1)} %bitcast.247, f32[512,6144]{1,0:T(8,128)} %get-tuple-element.96, f32[512]{0:T(512)S(1)} %get-tuple-element.95, bf16[1,128,3072]{2,1,0:T(8,128)(2,1)S(1)} %copy-done), kind=kOutput, calls=%fused_computation.16 | convolution fusion | flops 1219035136 | bytes 18089984 | tf_op jit(solution)/shard_map/dot_general | solution.py:95
  535.8 1.1 copy-done.3
  537.2 1.0 fusion.95
  538.1 1.3 fusion.75
  539.8 2.0 copy.17
  541.8 63.4 %reduce-scatter.11.cloned.1.call-done = bf16[32,3072]{1,0:T(8,128)(2,1)} async-done(((bf16[512,3072]{1,0:T(8,128)(2,1)}), bf16[32,3072]{1,0:T(8,128)(2,1)}) %reduce-scatter.11.cloned.1.call-update) | async-done | bytes 196624 | tf_op jit(solution)/shard_map/reduce_scatter | solution.py:94
  605.2 1.0 fusion.78
  606.2 1.0 maximum_bitcast_fusion.1
  (113 shorter events, 8.6 us)
Async XLA Ops:
  7.2 63.8 %copy-start = (bf16[1,128,3072]{2,1,0:T(8,128)(2,1)S(1)}, bf16[1,128,3072]{2,1,0:T(8,128)(2,1)}, u32[]{:S(2)}) copy-start(bf16[1,128,3072]{2,1,0:T(8,128)(2,1)} %param.17) | copy-start | bytes 2359300
  7.2 2.6 copy-start.8
  7.2 1.3 copy-start.17
  9.7 2.4 copy-start.22
  12.1 5.7 copy-start.32
  12.1 7.8 %copy-start.7 = (bf16[1,3072,3,128]{3,1,2,0:T(8,128)(2,1)S(1)}, bf16[1,3072,3,128]{3,1,2,0:T(8,128)(2,1)}, u32[]{:S(2)}) copy-start(bf16[1,3072,3,128]{3,1,2,0:T(8,128)(2,1)} %param.15) | copy-start | bytes 7077892
  12.1 48.0 %all-to-all-start = ((bf16[16,32,3072]{2,1,0:T(8,128)(2,1)}), bf16[16,32,3072]{2,1,0:T(8,128)(2,1)}, u32[]{:S(2)}, u32[]{:S(2)}) async-start(bf16[16,32,3072]{2,1,0:T(8,128)(2,1)} %stack.39), calls=%async_computation | async-start | bytes 6291456 | tf_op jit(solution)/shard_map/all_to_all | solution.py:17
  17.7 133.8 %reduce-scatter.5.cloned.1.call-start = ((), (), s32[]{:S(2)}) async-start(), calls=%async_computation.8 | async-start | bytes 3342336 | tf_op jit(solution)/shard_map/reduce_scatter | solution.py:94
  60.2 4.9 copy-start.1
  60.2 4.9 copy-start.16
  60.2 4.9 copy-start.28
  65.3 5.7 copy-start.9
  152.5 7.7 %collective-permute-start = (bf16[32,3072]{1,0:T(8,128)(2,1)S(1)}, bf16[32,3072]{1,0:T(8,128)(2,1)}, u32[]{:S(2)}, u32[]{:S(2)}) collective-permute-start(bf16[32,3072]{1,0:T(8,128)(2,1)S(1)} %fusion.39), channel_id=1, source_target_pairs={{0,16},{16,32},{32,48},{48,64},{64,80},{80,96},{96,112},{112,128},... | collective-permute-start | bytes 589832 | tf_op jit(solution)/shard_map/ppermute | solution.py:24
  164.3 46.7 %all-to-all-start.1 = ((bf16[16,32,3072]{2,1,0:T(8,128)(2,1)}), bf16[16,32,3072]{2,1,0:T(8,128)(2,1)}, u32[]{:S(2)}, u32[]{:S(2)}) async-start(bf16[16,32,3072]{2,1,0:T(8,128)(2,1)} %stack.41), calls=%async_computation.2 | async-start | bytes 6291456 | tf_op jit(solution)/shard_map/all_to_all | solution.py:17
  168.8 134.4 %reduce-scatter.7.cloned.1.call-start = ((), (), s32[]{:S(2)}) async-start(), calls=%async_computation.9 | async-start | bytes 3342336 | tf_op jit(solution)/shard_map/reduce_scatter | solution.py:94
  211.0 4.9 copy-start.10
  211.0 4.9 copy-start.29
  215.6 7.2 %copy-start.2 = (f32[512,3,1,128]{3,0,2,1:T(8,128)}, f32[512,3,1,128]{3,0,2,1:T(8,128)S(1)}, u32[]{:S(2)}) copy-start(f32[512,3,1,128]{3,0,2,1:T(8,128)S(1)} %fusion.16) | copy-start | bytes 2359300
  215.9 0.6 copy-start.24
  216.5 6.3 %copy-start.11 = (bf16[12,512,128]{2,1,0:T(8,128)(2,1)}, bf16[12,512,128]{2,1,0:T(8,128)(2,1)S(1)}, u32[]{:S(2)}) copy-start(bf16[12,512,128]{2,1,0:T(8,128)(2,1)S(1)} %get-tuple-element.72) | copy-start | bytes 4718596
  304.2 8.7 %copy-start.18 = (bf16[32,3072]{1,0:T(8,128)(2,1)}, bf16[32,3072]{1,0:T(8,128)(2,1)S(1)}, u32[]{:S(2)}) copy-start(bf16[32,3072]{1,0:T(8,128)(2,1)S(1)} %fusion.47) | copy-start | bytes 589828
  304.2 7.6 %collective-permute-start.1 = (bf16[32,3072]{1,0:T(8,128)(2,1)S(1)}, bf16[32,3072]{1,0:T(8,128)(2,1)S(1)}, u32[]{:S(2)}, u32[]{:S(2)}) collective-permute-start(bf16[32,3072]{1,0:T(8,128)(2,1)S(1)} %fusion.47), channel_id=1, source_target_pairs={{0,16},{16,32},{32,48},{48,64},{64,80},{80,96},{96,112},{112,128},... | collective-permute-start | bytes 589832 | tf_op jit(solution)/shard_map/ppermute | solution.py:24
  315.8 46.7 %all-to-all-start.2 = ((bf16[16,32,3072]{2,1,0:T(8,128)(2,1)}), bf16[16,32,3072]{2,1,0:T(8,128)(2,1)}, u32[]{:S(2)}, u32[]{:S(2)}) async-start(bf16[16,32,3072]{2,1,0:T(8,128)(2,1)} %stack.43), calls=%async_computation.4 | async-start | bytes 6291456 | tf_op jit(solution)/shard_map/all_to_all | solution.py:17
  320.3 134.4 %reduce-scatter.9.cloned.1.call-start = ((), (), s32[]{:S(2)}) async-start(), calls=%async_computation.10 | async-start | bytes 3342336 | tf_op jit(solution)/shard_map/reduce_scatter | solution.py:94
  362.5 4.9 copy-start.12
  362.5 4.9 copy-start.30
  367.1 7.2 %copy-start.4 = (f32[512,3,1,128]{3,0,2,1:T(8,128)}, f32[512,3,1,128]{3,0,2,1:T(8,128)S(1)}, u32[]{:S(2)}) copy-start(f32[512,3,1,128]{3,0,2,1:T(8,128)S(1)} %fusion.19) | copy-start | bytes 2359300
  367.4 0.6 copy-start.26
  368.0 6.3 %copy-start.13 = (bf16[12,512,128]{2,1,0:T(8,128)(2,1)}, bf16[12,512,128]{2,1,0:T(8,128)(2,1)S(1)}, u32[]{:S(2)}) copy-start(bf16[12,512,128]{2,1,0:T(8,128)(2,1)S(1)} %get-tuple-element.70) | copy-start | bytes 4718596
  455.7 8.7 %copy-start.20 = (bf16[32,3072]{1,0:T(8,128)(2,1)}, bf16[32,3072]{1,0:T(8,128)(2,1)S(1)}, u32[]{:S(2)}) copy-start(bf16[32,3072]{1,0:T(8,128)(2,1)S(1)} %fusion.52) | copy-start | bytes 589828
  455.7 7.6 %collective-permute-start.2 = (bf16[32,3072]{1,0:T(8,128)(2,1)S(1)}, bf16[32,3072]{1,0:T(8,128)(2,1)S(1)}, u32[]{:S(2)}, u32[]{:S(2)}) collective-permute-start(bf16[32,3072]{1,0:T(8,128)(2,1)S(1)} %fusion.52), channel_id=1, source_target_pairs={{0,16},{16,32},{32,48},{48,64},{64,80},{80,96},{96,112},{112,128},... | collective-permute-start | bytes 589832 | tf_op jit(solution)/shard_map/ppermute | solution.py:24
  467.3 46.7 %all-to-all-start.3 = ((bf16[16,32,3072]{2,1,0:T(8,128)(2,1)}), bf16[16,32,3072]{2,1,0:T(8,128)(2,1)}, u32[]{:S(2)}, u32[]{:S(2)}) async-start(bf16[16,32,3072]{2,1,0:T(8,128)(2,1)} %stack.45), calls=%async_computation.6 | async-start | bytes 6291456 | tf_op jit(solution)/shard_map/all_to_all | solution.py:17
  471.8 133.4 %reduce-scatter.11.cloned.1.call-start = ((), (), s32[]{:S(2)}) async-start(), calls=%async_computation.11 | async-start | bytes 3342336 | tf_op jit(solution)/shard_map/reduce_scatter | solution.py:94
  514.0 4.9 copy-start.14
  514.0 4.9 copy-start.31
  518.5 6.3 %copy-start.6 = (f32[512,3,1,128]{3,0,2,1:T(8,128)}, f32[512,3,1,128]{3,0,2,1:T(8,128)S(1)}, u32[]{:S(2)}) copy-start(f32[512,3,1,128]{3,0,2,1:T(8,128)S(1)} %fusion.22) | copy-start | bytes 2359300
  519.1 5.7 copy-start.15
  535.8 1.1 copy-start.3
  535.8 1.4 copy-start.5
  535.8 2.4 copy-start.25
  535.8 2.4 copy-start.27
  539.5 65.7 %copy-start.23 = (f32[1,3072]{1,0:T(1,128)S(1)}, f32[1,3072]{1,0:T(1,128)}, u32[]{:S(2)}) copy-start(f32[1,3072]{1,0:T(1,128)} %get-tuple-element.73) | copy-start | bytes 36868
  539.5 66.7 %copy-start.19 = (bf16[32,3072]{1,0:T(8,128)(2,1)S(1)}, bf16[32,3072]{1,0:T(8,128)(2,1)}, u32[]{:S(2)}) copy-start(bf16[32,3072]{1,0:T(8,128)(2,1)} %copy-done.18) | copy-start | bytes 589828
  539.5 66.7 %copy-start.21 = (bf16[32,3072]{1,0:T(8,128)(2,1)S(1)}, bf16[32,3072]{1,0:T(8,128)(2,1)}, u32[]{:S(2)}) copy-start(bf16[32,3072]{1,0:T(8,128)(2,1)} %copy-done.20) | copy-start | bytes 589828
Sparse Core Ops, SparseCore 0:
  82.1 69.3 reduce-scatter.4
  233.9 69.2 reduce-scatter.6
  385.4 69.2 reduce-scatter.8
  535.9 69.2 reduce-scatter.10
